TPU v7x, 256 devices: a whole 4x4x8 slice. The times are simulated.
256 devices in a mesh: freq: 8 (over y, core), se: 32 (over z, x).
Axes of the slice: x: 4, y: 4, z: 8, core: 2. Of those that a mesh axis runs over, the one named last changes fastest.
Arguments:
- stress_modes: bfloat16 [262144, 800], P('se', 'freq'), may hold values from -6 to 6
- modal_transfer: bfloat16 [800, 48, 128], P('se', 'freq'), may hold values from -0.21875 to 0.21875
- input_psd: bfloat16 [48, 64, 128], P('freq'), as said below
- panel_super: int32 [1024, 1], replicated, may hold values from 0 to 31; in each aligned block of 32 rows (0 to 31, 32 to 63, ...) at most 2 rows name the same one
- panel_offset: int32 [1024], replicated, may hold values from 0 to 8128
- panel_count: int32 [1024], replicated, may hold values from 1 to 64, 49152 in all
Outputs:
- cross_spectra: bfloat16 [1024, 48, 64, 128], P('se', 'freq')
Inputs may be any that keep to these rules, and one draw needn't show every extreme that they name: `panel_super`: among the monitored panels of each owner (the 32 consecutive entries of one block) at most 2 lie on one superelement. `input_psd`: each matrix is Hermitian positive definite.
All inputs are finite; a program needn't handle non-finite values.
Results may differ from a plain program's by a relative error of at most 0.0056.
Values may be sent and summed in bfloat16 or wider, within the bound.
A program may use at most 64 MiB of HBM per device.

v0:
```python
import jax
import jax.numpy as jnp
from jax import lax
from jax.sharding import PartitionSpec as P

MODES = 800
NI = 64
PROW = 64
FREQ_DEV = 6
PAN_DEV = 32


def per_device(stress_modes, modal_transfer, input_psd, panel_super, panel_offset, panel_count):
    owners_count = lax.axis_size("se")
    myself = lax.axis_index("se")
    capacity = max(2, (2 * PAN_DEV + owners_count - 1) // owners_count)
    local_modes = stress_modes.shape[1]
    owners = panel_super[:, 0].reshape(owners_count, PAN_DEV)
    offsets = panel_offset.reshape(owners_count, PAN_DEV)
    counts = panel_count.reshape(owners_count, PAN_DEV)
    zero = jnp.zeros((), jnp.bfloat16)
    held = (owners == myself).astype(jnp.int32)
    ranks = jnp.cumsum(held, axis=1) - 1
    slot_ids = jnp.arange(capacity, dtype=jnp.int32)
    picks = held[:, None, :] * (ranks[:, None, :] == slot_ids[None, :, None]).astype(jnp.int32)
    first_rows = jnp.sum(picks * offsets[:, None, :], axis=2)
    filled = jnp.sum(picks, axis=2)
    row_index = first_rows[:, :, None] + jnp.arange(PROW, dtype=jnp.int32)[None, None, :]
    outgoing = jnp.take(stress_modes, row_index.reshape(-1), axis=0)
    outgoing = outgoing.reshape(owners_count, capacity, PROW, local_modes)
    outgoing = jnp.where(filled[:, :, None, None] > 0, outgoing, zero)
    my_owners = lax.dynamic_slice_in_dim(owners, myself, 1, 0)[0]
    my_counts = lax.dynamic_slice_in_dim(counts, myself, 1, 0)[0]
    positions = jnp.arange(PAN_DEV, dtype=jnp.int32)
    earlier = (my_owners[None, :] == my_owners[:, None]) & (positions[None, :] < positions[:, None])
    my_ranks = jnp.sum(earlier.astype(jnp.int32), axis=1)
    my_slots = my_owners * capacity + my_ranks
    live = jnp.arange(PROW, dtype=jnp.int32)[None, :] < my_counts[:, None]
    whole_transfer = lax.all_gather(modal_transfer, "se", axis=0, tiled=True)
    flat = whole_transfer.reshape(MODES, FREQ_DEV * 2 * NI)
    full_rows = lax.all_gather(outgoing, "freq", axis=3, tiled=True)
    response = jnp.dot(
        full_rows.reshape(-1, MODES), flat, preferred_element_type=jnp.float32
    ).astype(jnp.bfloat16)
    response = response.reshape(owners_count, capacity * PROW, FREQ_DEV * 2 * NI)
    incoming = lax.all_to_all(response, "se", split_axis=0, concat_axis=0, tiled=True)
    picked = jnp.take(
        incoming.reshape(owners_count * capacity, PROW, FREQ_DEV * 2 * NI), my_slots, axis=0
    )
    picked = jnp.where(live[:, :, None], picked, zero)
    response = picked.reshape(PAN_DEV, PROW, FREQ_DEV, 2 * NI)
    real_part = input_psd[:, :, :NI]
    imag_part = input_psd[:, :, NI:]
    upper = jnp.concatenate([real_part, imag_part], axis=2)
    lower = jnp.concatenate([-imag_part, real_part], axis=2)
    block = jnp.concatenate([upper, lower], axis=1)
    mixed = jnp.einsum(
        "prfc,fcd->prfd", response, block, preferred_element_type=jnp.float32
    ).astype(jnp.bfloat16)
    turned = jnp.concatenate([mixed[..., NI:], -mixed[..., :NI]], axis=3)
    cross_real = jnp.einsum("pifc,pjfc->pfij", mixed, response, preferred_element_type=jnp.float32)
    cross_imag = jnp.einsum("pifc,pjfc->pfij", turned, response, preferred_element_type=jnp.float32)
    return jnp.concatenate([cross_real, cross_imag], axis=3).astype(jnp.bfloat16)


def solution(mesh):
    in_specs = (P("se", "freq"), P("se", "freq", None), P("freq", None, None), P(), P(), P())
    out_specs = P("se", "freq", None, None)
    return jax.shard_map(
        per_device, mesh=mesh, in_specs=in_specs, out_specs=out_specs, check_vma=False
    )
```

profile of v0, /device:TPU:1, one launch (start us, length us, event | category | flops | bytes accessed | tf_op | source)
XLA Modules:
  0.0 376.3 jit_solution(13225291655107222641)
XLA Ops:
  6.5 1.4 copy.43
  8.0 0.5 broadcast.125
  8.6 1.3 reduce.3
  10.0 0.2 reduce_window_sum.11
  10.2 0.8 mul.44
  10.9 0.1 select_reduce_fusion
  11.2 0.1 iota_add_fusion
  11.3 0.1 add.102
  11.4 3.2 copy.40
  14.6 12.1 %gather_fusion = bf16[4096,100]{1,0:T(8,128)(2,1)S(1)} fusion(bf16[8192,100]{1,0:T(8,128)(2,1)S(1)} %copy.40, s32[4096]{0:T(1024)S(1)} %broadcast_clamp_fusion), kind=kCustom, calls=%fused_computation | custom fusion | bytes 1654784 | tf_op jit(solution)/shard_map/jit(_take)/gather | solution.py:29
  26.8 2.6 copy.41
  29.4 0.1 compare_and_fusion
  29.6 1.4 select_select_fusion.1
  31.0 55.9 %all-gather.5.cloned.1.call-done = bf16[800,6,128]{2,1,0:T(8,128)(2,1)} async-done(((bf16[25,6,128]{2,1,0:T(8,128)(2,1)}), bf16[800,6,128]{2,1,0:T(8,128)(2,1)}) %all-gather.5.cloned.1.call-update) | async-done | bytes 1228816 | tf_op jit(solution)/shard_map/all_gather | solution.py:39
  86.9 2.8 copy.44
  89.7 73.3 %all-gather.3.cloned.1.call-done = bf16[32,2,64,800]{2,0,1,3:T(8,128)(2,1)} async-done(((bf16[32,2,64,100]{2,0,1,3:T(8,128)(2,1)}), bf16[32,2,64,800]{2,0,1,3:T(8,128)(2,1)}) %all-gather.3.cloned.1.call-update) | async-done | bytes 6553616 | tf_op jit(solution)/shard_map/all_gather | solution.py:41
  163.0 18.3 %copy.42 = bf16[32,2,64,800]{3,2,1,0:T(8,128)(2,1)} copy(bf16[32,2,64,800]{2,0,1,3:T(8,128)(2,1)} %all-gather.3.cloned.1.call-done) | data formatting | bytes 13107200 | tf_op jit(solution)/shard_map/all_gather | solution.py:41
  181.3 11.6 %convolution_convert_fusion = bf16[4096,768]{1,0:T(8,128)(2,1)} fusion(bf16[4096,800]{1,0:T(8,128)(2,1)} %bitcast.30, bf16[800,768]{0,1:T(8,128)(2,1)S(1)} %bitcast.33), kind=kOutput, calls=%fused_computation.2 | convolution fusion | flops 5036310528 | bytes 14073856 | tf_op jit(solution)/shard_map/dot_general | solution.py:42
  192.9 10.0 %all-to-all-start = ((bf16[32,128,768]{2,1,0:T(8,128)(2,1)}), bf16[32,128,768]{2,1,0:T(8,128)(2,1)}, u32[]{:S(2)}, u32[]{:S(2)}) async-start(bf16[32,128,768]{2,1,0:T(8,128)(2,1)} %bitcast.31), calls=%async_computation | async-start | bytes 12582912 | tf_op jit(solution)/shard_map/all_to_all | solution.py:46
  203.0 0.2 convert_reduce_fusion
  203.3 0.1 slice_negate_fusion.1
  203.4 140.3 %all-to-all-done = bf16[32,128,768]{2,1,0:T(8,128)(2,1)} async-done(((bf16[32,128,768]{2,1,0:T(8,128)(2,1)}), bf16[32,128,768]{2,1,0:T(8,128)(2,1)}, u32[]{:S(2)}, u32[]{:S(2)}) %all-to-all-start) | async-done | bytes 6291488 | tf_op jit(solution)/shard_map/all_to_all | solution.py:46
  343.7 3.5 gather_fusion.1
  347.2 4.7 %gather.15 = bf16[32,64,6,128]{3,2,1,0:T(8,128)(2,1)} reshape(bf16[32,64,768]{2,1,0:T(8,128)(2,1)S(1)} %gather_fusion.1) | data formatting | bytes 6291456 | tf_op jit(solution)/shard_map/jit(_take)/gather | solution.py:47
  351.9 6.1 %select_select_fusion = bf16[32,64,6,128]{3,2,1,0:T(8,128)(2,1)S(1)} fusion(bf16[32,64,6,128]{3,2,1,0:T(8,128)(2,1)} %gather.15, pred[32]{0:T(512)(128)(4,1)S(1)} %compare_and_fusion.1, pred[32,64]{1,0:T(8,128)(4,1)S(1)} %iota_compare_fusion.2), kind=kLoop, calls=%fused_computation.3 | loop fusion | flops 3145728 | bytes 6293536 | tf_op jit(solution)/shard_map/jit(_where)/select_n | solution.py:50
  358.0 0.9 copy.45
  358.8 1.0 fusion.12
  359.9 0.8 convert_bitcast_fusion
  360.7 1.8 fusion.4
  362.5 1.2 fusion.23
  363.7 2.4 fusion.7
  366.1 3.4 pad_maximum_fusion.1
  (22 shorter events, 0.5 us)
Async XLA Ops:
  6.5 80.3 %all-gather.5.cloned.1.call-start = ((), (), s32[]{:S(2)}) async-start(), calls=%async_computation.2 | async-start | bytes 1689600 | tf_op jit(solution)/shard_map/all_gather | solution.py:39
  8.0 155.0 %all-gather.3.cloned.1.call-start = ((), (), s32[]{:S(2)}) async-start(), calls=%async_computation.1 | async-start | bytes 14745600 | tf_op jit(solution)/shard_map/all_gather | solution.py:41
  192.9 10.0 %copy-start.1 = (s32[1024]{0:T(1024)S(1)}, s32[1024]{0:T(1024)}, u32[]{:S(2)}) copy-start(s32[1024]{0:T(1024)} %param.11) | copy-start | bytes 12292
  192.9 10.4 %copy-start = (bf16[6,64,128]{2,1,0:T(8,128)(2,1)S(1)}, bf16[6,64,128]{2,1,0:T(8,128)(2,1)}, u32[]{:S(2)}) copy-start(bf16[6,64,128]{2,1,0:T(8,128)(2,1)} %param.8) | copy-start | bytes 294916
  192.9 150.8 %all-to-all-start = ((bf16[32,128,768]{2,1,0:T(8,128)(2,1)}), bf16[32,128,768]{2,1,0:T(8,128)(2,1)}, u32[]{:S(2)}, u32[]{:S(2)}) async-start(bf16[32,128,768]{2,1,0:T(8,128)(2,1)} %bitcast.31), calls=%async_computation | async-start | bytes 12582912 | tf_op jit(solution)/shard_map/all_to_all | solution.py:46
Sparse Core Ops, SparseCore 0:
  10.0 76.8 all-gather.4
  88.7 74.2 all-gather.2
where the time goes:
time: 381 us; the launch traced here: 376 us
  waiting for transfers between devices  269 us (71%)
  local copies, waits for them, and re-layouts  51.2 us (13%)
  matrix products  16.8 us (4%)
  other arithmetic  15.2 us (4%)
  between operations  13.6 us (4%)
  starting transfers between devices  10 us (3%)
    all_to_all x1, waiting for transfers between devices, per_device(): lax.all_to_all(response, 'se', split_axis=0, concat_axis=0, tiled=True)  140 us
    all_gather x1, waiting for transfers between devices, per_device(): full_rows = lax.all_gather(outgoing, 'freq', axis=3, tiled=True)  73.3 us
    all_gather x1, waiting for transfers between devices, per_device(): whole_transfer = lax.all_gather(modal_transfer, 'se', axis=0, tiled=True)  55.9 us
    all_gather x1, local copies, waits for them, and re-layouts, per_device(): full_rows = lax.all_gather(outgoing, 'freq', axis=3, tiled=True)  18.3 us
    gather x2, local copies, waits for them, and re-layouts, per_device(): outgoing = jnp.take(stress_modes, row_index.reshape(-1), axis=0)  14.8 us
    dot_general x1, matrix products, per_device(): jnp.dot(full_rows.reshape(-1, MODES), flat, preferred_element_type=jnp.fl...  11.6 us
    all_to_all x1, starting transfers between devices, per_device(): lax.all_to_all(response, 'se', split_axis=0, concat_axis=0, tiled=True)  9.97 us
    gather x2, local copies, waits for them, and re-layouts, per_device(): jnp.take(incoming.reshape(owners_count * capacity, PROW, FREQ_DEV * 2 * N...  8.22 us
  transfers between devices with their start and end apart: 3, of which 3 were waited for; matrix products, arithmetic and copies ran while one was open for 7% of the time, Pallas kernels for 0%

commit v1 on v0

v1 whole, which is shorter than its diff:
```python
import functools

import jax
import jax.numpy as jnp
from jax import lax
from jax.experimental import pallas as pl
from jax.experimental.pallas import tpu as pltpu
from jax.sharding import PartitionSpec as P

MESH = pl.DeviceIdType.MESH
MODES = 800
NI = 64
PROW = 64
FREQ_DEV = 6
PAN_DEV = 32
NF = 8
NZ = 8
NX = 4
NS = NZ * NX
LOCAL = MODES // NF
SHARD = MODES // NS
CHUNKS = ((0, 48), (48, 32), (80, 32))
PADDED = 112
LANES = PAN_DEV * PROW
WIDE = FREQ_DEV * 2 * NI
TSH = 32
f32 = jnp.float32
bf16 = jnp.bfloat16


def div(a, b):
    return lax.div(a, jnp.int32(b))


def rem(a, b):
    return lax.rem(a, jnp.int32(b))


def response_kernel(
    sup_hbm, off_hbm, cnt_hbm, table_hbm, t_hbm, psd_hbm, resp_ref, blocks_ref,
    sup, off, cnt, t_ref, psd_ref, in_sem, table, send_buf, rb0, rb1, rb2, xb0, xb1, xb2, tbuf, tin, acc, tt, perm,
    ranks, table_sem, a2a_send, a2a_recv, y_send, y_recv, tz_send, tz_recv, tx_send, tx_recv,
):
    rbs, xbs = (rb0, rb1, rb2), (xb0, xb1, xb2)
    f = lax.axis_index("freq")
    me = lax.axis_index("se")
    z, x = div(me, NX), rem(me, NX)
    up, down = rem(f + 2, NF), rem(f + NF - 2, NF)
    across = rem(f + 4, NF)
    twin = f + 1 - 2 * rem(f, 2)
    x_up = z * NX + rem(x + 1, NX)
    x_down = z * NX + rem(x + NX - 1, NX)

    small = [
        pltpu.make_async_copy(source, to, in_sem.at[k])
        for k, (source, to) in enumerate(
            ((t_hbm, t_ref), (sup_hbm, sup), (off_hbm, off), (cnt_hbm, cnt), (psd_hbm, psd_ref))
        )
    ]
    for copy in small:
        copy.start()
    tiles = table.shape[0]

    @pl.loop(0, tiles)
    def _(t):
        part = table_hbm.at[:, pl.ds(pl.multiple_of(t * 128, 128), 128)]
        pltpu.make_async_copy(part, table.at[t], table_sem).start()

    barrier = pltpu.get_barrier_semaphore()

    @pl.loop(1, NS)
    def _(i):
        pl.semaphore_signal(barrier, 1, device_id={"se": rem(me + i, NS)}, device_id_type=MESH)

    for g in (up, down, twin):
        pl.semaphore_signal(barrier, 1, device_id={"freq": g}, device_id_type=MESH)

    tin[...] = jnp.zeros_like(tin)
    small[0].wait()
    tin[:, 0:SHARD, :] = t_ref[...]
    tbuf[x, z] = tin[...]
    send_buf[:, PADDED - 16 : PADDED, :] = jnp.zeros((NS, 16, 128), bf16)

    pl.semaphore_wait(barrier, NS - 1 + 3)

    def tz_copy(i):
        return pltpu.make_async_remote_copy(
            src_ref=tbuf.at[x, z], dst_ref=tbuf.at[x, z], send_sem=tz_send, recv_sem=tz_recv,
            device_id={"se": rem(z + i, NZ) * NX + x}, device_id_type=MESH,
        )

    @pl.loop(1, NZ)
    def _(i):
        tz_copy(i).start()

    small[1].wait()
    small[2].wait()
    pltpu.make_async_copy(table, table, table_sem).wait()

    lane = lax.broadcasted_iota(jnp.int32, (LOCAL, 128), 1)

    def window(start, place):
        tile = div(start, 128)
        inside = start - tile * 128
        a = table[tile].astype(f32)
        b = table[jnp.minimum(tile + 1, tiles - 1)].astype(f32)
        both = jnp.where(lane >= inside, a, b)
        return pltpu.roll(both, rem(place + 128 - inside, 128), 1)

    def gather(o):
        base = o * PAN_DEV
        first, last = jnp.int32(0), jnp.int32(0)
        hits = [sup[base + j] == me for j in range(PAN_DEV)]
        starts = [off[base + j] for j in range(PAN_DEV)]
        for j in range(PAN_DEV):
            last = jnp.where(hits[j], starts[j], last)
            k = PAN_DEV - 1 - j
            first = jnp.where(hits[k], starts[k], first)
        got = jnp.where(lane < PROW, window(first, 0), window(last, PROW)).astype(bf16)
        send_buf[o, 0:LOCAL, :] = got

    def a2a_copy(c, o):
        r0, rows = CHUNKS[c]
        return pltpu.make_async_remote_copy(
            src_ref=send_buf.at[o, pl.ds(r0, rows)], dst_ref=rbs[c].at[me],
            send_sem=a2a_send.at[c], recv_sem=a2a_recv.at[c],
            device_id={"se": o}, device_id_type=MESH,
        )

    @pl.loop(1, NS)
    def _(i):
        o = rem(me + i, NS)
        gather(o)
        a2a_copy(0, o).start()

    for c in range(1, len(CHUNKS)):

        @pl.loop(1, NS)
        def _(i):
            a2a_copy(c, rem(me + i, NS)).start()

    gather(me)
    for c, (r0, rows) in enumerate(CHUNKS):
        rbs[c][me] = send_buf[me, r0 : r0 + rows, :]

    def tz_all():
        return pltpu.make_async_copy(tbuf.at[0, 0 : NZ - 1], tbuf.at[0, 0 : NZ - 1], tz_recv)

    def tx_copy(k):
        if k < 2:
            source, to = tbuf.at[x], (x_up, x_down)[k]
        elif k == 2:
            source, to = tbuf.at[rem(x + NX - 1, NX), 0 : NZ // 2], x_up
        else:
            source, to = tbuf.at[rem(x + 1, NX), NZ // 2 : NZ], x_down
        return pltpu.make_async_remote_copy(
            src_ref=source, dst_ref=source, send_sem=tx_send.at[k], recv_sem=tx_recv.at[k],
            device_id={"se": to}, device_id_type=MESH,
        )

    tz_all().wait()
    tx_copy(0).start()
    tx_copy(1).start()

    small[3].wait()
    small[4].wait()
    half_lane = lax.broadcasted_iota(jnp.int32, (NI, 128), 1)
    for g in range(FREQ_DEV):
        turned = pltpu.roll(psd_ref[g].astype(f32), NI, 1)
        blocks_ref[g, 0:NI, :] = psd_ref[g]
        blocks_ref[g, NI:128, :] = jnp.where(half_lane < NI, -turned, turned).astype(bf16)

    mine = me * PAN_DEV
    own = [sup[mine + p] for p in range(PAN_DEV)]
    for p in range(PAN_DEV):
        rank = jnp.int32(0)
        for e in range(p):
            rank = jnp.where(own[e] == own[p], 1, rank)
        ranks[p] = rank

    row = lax.broadcasted_iota(jnp.int32, (128, 1), 0)
    column = lax.broadcasted_iota(jnp.int32, (128, PADDED * NF), 1)

    @pl.loop(0, NS * TSH // 128)
    def _(b):
        at = row + b * 128
        shard = div(at, TSH)
        place = rem(at, TSH)
        of_z, of_x = rem(shard, NZ), div(shard, NZ)
        mode = of_x * SHARD + place
        target = jnp.full((128, 1), -1, jnp.int32)
        for r0, rows in CHUNKS:
            inside = (mode >= r0) & (mode < r0 + rows)
            target = jnp.where(inside, r0 * NF + of_z * rows + mode - r0, target)
        target = jnp.where(place < SHARD, target, -1)
        perm[pl.ds(pl.multiple_of(b * 128, 128), 128), :] = jnp.where(column == target, 1.0, 0.0).astype(bf16)

    def select(c):
        rows = CHUNKS[c][1]
        all_c = rbs[c].at[0 : NS - 1]
        pltpu.make_async_copy(all_c, all_c, a2a_recv.at[c]).wait()
        at = lax.broadcasted_iota(jnp.int32, (rows, 128), 1)

        @pl.loop(0, PAN_DEV // 2)
        def _(q):
            p = 2 * q
            left = rbs[c][sup[mine + p]].astype(f32)
            right = rbs[c][sup[mine + p + 1]].astype(f32)
            left = pltpu.roll(left, PROW * ranks[p], 1)
            right = pltpu.roll(right, PROW * (1 - ranks[p + 1]), 1)
            live = jnp.where(at < PROW, cnt[mine + p], cnt[mine + p + 1] + PROW)
            pair = jnp.where(at < live, jnp.where(at < PROW, left, right), 0.0)
            xbs[c][f, :, pl.ds(pl.multiple_of(q * 128, 128), 128)] = pair.astype(bf16)

    def y_copy(c, k):
        xb = xbs[c]
        half = LANES // 2
        source, to = (
            (xb.at[f], up),
            (xb.at[f], down),
            (xb.at[down, :, 0:half], up),
            (xb.at[up, :, half:LANES], down),
            (xb.at[f], twin),
            (xb.at[down], twin),
            (xb.at[up], twin),
            (xb.at[across], twin),
        )[k]
        return pltpu.make_async_remote_copy(
            src_ref=source, dst_ref=source, send_sem=y_send.at[c, k], recv_sem=y_recv.at[c, k],
            device_id={"freq": to}, device_id_type=MESH,
        )

    def y_begin(c):
        for k in (0, 1, 4):
            y_copy(c, k).start()

    def y_forward(c):
        y_copy(c, 0).wait_recv()
        y_copy(c, 2).start()
        y_copy(c, 5).start()
        y_copy(c, 1).wait_recv()
        y_copy(c, 3).start()
        y_copy(c, 6).start()

    def y_last(c):
        y_copy(c, 2).wait_recv()
        y_copy(c, 3).wait_recv()
        y_copy(c, 7).start()

    def y_end(c):
        for k in (4, 5, 6, 7):
            y_copy(c, k).wait_recv()

    def multiply(c):
        r0, rows = CHUNKS[c]
        deep = rows * NF
        step = 256

        @pl.loop(0, LANES // step)
        def _(n):
            at = pl.ds(pl.multiple_of(n * step, step), step)
            block = xbs[c][:, :, at].reshape(deep, step)
            part = jnp.dot(tt[:, r0 * NF : r0 * NF + deep], block, preferred_element_type=f32)
            if c > 0:
                part = part + acc[:, at]
            if c < len(CHUNKS) - 1:
                acc[:, at] = part
            else:
                resp_ref[:, at] = part.astype(bf16)

    select(0)
    y_begin(0)
    tx_copy(0).wait_recv()
    tx_copy(2).start()
    tx_copy(1).wait_recv()
    tx_copy(3).start()
    y_forward(0)
    tx_copy(2).wait_recv()
    tx_copy(3).wait_recv()
    for g in range(FREQ_DEV):
        block = tbuf[:, :, g].reshape(NS * TSH, 128)
        tt[g * 128 : (g + 1) * 128, :] = lax.dot_general(
            block, perm[...], (((0,), (0,)), ((), ())), preferred_element_type=f32
        ).astype(bf16)
    y_last(0)
    select(1)
    y_begin(1)
    y_end(0)
    multiply(0)
    y_forward(1)
    y_last(1)
    select(2)
    y_begin(2)
    y_end(1)
    multiply(1)
    y_forward(2)
    y_last(2)
    y_end(2)
    multiply(2)

    sent = tbuf.at[0, 0 : NZ - 1]
    pltpu.make_async_copy(sent, sent, tz_send).wait()
    for k in range(4):
        tx_copy(k).wait_send()
    for c in range(len(CHUNKS)):
        sent = rbs[c].at[0 : NS - 1]
        pltpu.make_async_copy(sent, sent, a2a_send.at[c]).wait()
        for k in range(8):
            y_copy(c, k).wait_send()


def responses(sup, off, cnt, table, transfer, psd):
    return pl.pallas_call(
        response_kernel,
        out_shape=[
            jax.ShapeDtypeStruct((WIDE, LANES), bf16),
            jax.ShapeDtypeStruct((FREQ_DEV, 128, 128), bf16),
        ],
        in_specs=[pl.BlockSpec(memory_space=pltpu.HBM)] * 6,
        out_specs=[pl.BlockSpec(memory_space=pltpu.VMEM)] * 2,
        scratch_shapes=[
            *[pltpu.SMEM(a.shape, jnp.int32) for a in (sup, off, cnt)],
            pltpu.VMEM(transfer.shape, bf16),
            pltpu.VMEM(psd.shape, bf16),
            pltpu.SemaphoreType.DMA((5,)),
            pltpu.VMEM((table.shape[1] // 128, LOCAL, 128), bf16),
            pltpu.VMEM((NS, PADDED, 128), bf16),
            *[pltpu.VMEM((NS, rows, 128), bf16) for _, rows in CHUNKS],
            *[pltpu.VMEM((NF, rows, LANES), bf16) for _, rows in CHUNKS],
            pltpu.VMEM((NX, NZ, FREQ_DEV, TSH, 128), bf16),
            pltpu.VMEM((FREQ_DEV, TSH, 128), bf16),
            pltpu.VMEM((WIDE, LANES), f32),
            pltpu.VMEM((WIDE, PADDED * NF), bf16),
            pltpu.VMEM((NS * TSH, PADDED * NF), bf16),
            pltpu.SMEM((PAN_DEV,), jnp.int32),
            pltpu.SemaphoreType.DMA,
            pltpu.SemaphoreType.DMA((len(CHUNKS),)),
            pltpu.SemaphoreType.DMA((len(CHUNKS),)),
            pltpu.SemaphoreType.DMA((len(CHUNKS), 8)),
            pltpu.SemaphoreType.DMA((len(CHUNKS), 8)),
            pltpu.SemaphoreType.DMA,
            pltpu.SemaphoreType.DMA,
            pltpu.SemaphoreType.DMA((4,)),
            pltpu.SemaphoreType.DMA((4,)),
        ],
        compiler_params=pltpu.CompilerParams(
            collective_id=0, has_side_effects=True, vmem_limit_bytes=44 * 2**20
        ),
        name="responses",
    )(*[pltpu.with_memory_space_constraint(a, pltpu.HBM) for a in (sup, off, cnt, table, transfer, psd)])


def spectra_kernel(resp_ref, blocks, out_ref):
    lane = lax.broadcasted_iota(jnp.int32, (NI, 128), 1)

    for g in range(FREQ_DEV):
        for h in range(2):
            resp = resp_ref[g * 128 : (g + 1) * 128, h * 128 : (h + 1) * 128]
            mixed = lax.dot_general(
                resp, blocks[g], (((0,), (0,)), ((), ())), preferred_element_type=f32
            ).astype(bf16)
            turned = jnp.concatenate([-resp[NI:], resp[:NI]], axis=0)
            both = jnp.concatenate([resp, turned], axis=1)
            cross = jnp.dot(mixed, both, preferred_element_type=f32)
            real, imag = cross[:, 0:128], cross[:, 128:256]
            out_ref[2 * h, g] = jnp.where(lane < NI, real[0:NI], pltpu.roll(imag[0:NI], NI, 1)).astype(bf16)
            out_ref[2 * h + 1, g] = jnp.where(lane < NI, pltpu.roll(real[NI:], NI, 1), imag[NI:]).astype(bf16)


def spectra(resp, blocks):
    step = 256
    return pl.pallas_call(
        spectra_kernel,
        grid=(LANES // step,),
        out_shape=jax.ShapeDtypeStruct((PAN_DEV, FREQ_DEV, PROW, 2 * NI), bf16),
        in_specs=[
            pl.BlockSpec((WIDE, step), lambda i: (0, i)),
            pl.BlockSpec((FREQ_DEV, 128, 128), lambda i: (0, 0, 0)),
        ],
        out_specs=pl.BlockSpec((step // PROW, FREQ_DEV, PROW, 2 * NI), lambda i: (i, 0, 0, 0)),
        name="spectra",
    )(resp, blocks)


def per_device(stress_modes, modal_transfer, input_psd, panel_super, panel_offset, panel_count):
    resp, blocks = responses(
        panel_super.reshape(-1), panel_offset, panel_count,
        stress_modes.T, modal_transfer.transpose(1, 0, 2), input_psd,
    )
    return spectra(resp, blocks)


def solution(mesh):
    in_specs = (P("se", "freq"), P("se", "freq", None), P("freq", None, None), P(), P(), P())
    out_specs = P("se", "freq", None, None)
    return jax.shard_map(
        per_device, mesh=mesh, in_specs=in_specs, out_specs=out_specs, check_vma=False
    )
```

time: 381 us -> 82.8 us (0.22); the launches traced: 376 us -> 82.6 us
  waiting for transfers between devices: 269 us -> 0 us
  Pallas kernels: 0 us -> 80.3 us
  local copies, waits for them, and re-layouts: 51.2 us -> 2.32 us
  matrix products: 16.8 us -> 0 us
  other arithmetic: 15.2 us -> 0 us
  between operations: 13.6 us -> 0.02 us
  starting transfers between devices: 10 us -> 0 us
    all_to_all x1 -> x0, waiting for transfers between devices: 140 us -> none  [per_device(): lax.all_to_all(response, 'se', split_axis=0, concat_axis=0, tiled=True)]
    all_gather x2 -> x0, waiting for transfers between devices: 129 us -> none  [the longest x1 73.3 us: per_device(): full_rows = lax.all_gather(outgoing, 'freq', axis=3, tiled=True)]
    pallas_call x0 -> x2, Pallas kernels: none -> 80.3 us  [the longest x1 68.3 us: responses(): pl.pallas_call(response_kernel, out_shape=[jax.ShapeDtypeStruct((WIDE, LA...]
    gather x4 -> x0, local copies, waits for them, and re-layouts: 23 us -> none  [the longest x2 14.8 us: per_device(): outgoing = jnp.take(stress_modes, row_index.reshape(-1), axis=0)]
    all_gather x2 -> x0, local copies, waits for them, and re-layouts: 21.1 us -> none  [the longest x1 18.3 us: per_device(): full_rows = lax.all_gather(outgoing, 'freq', axis=3, tiled=True)]
    dot_general x3 -> x0, matrix products: 15.7 us -> none  [the longest x1 11.6 us: per_device(): jnp.dot(full_rows.reshape(-1, MODES), flat, preferred_element_type=jnp.fl...]
    all_to_all x1 -> x0, starting transfers between devices: 9.97 us -> none  [per_device(): lax.all_to_all(response, 'se', split_axis=0, concat_axis=0, tiled=True)]
    select_n x4 -> x0, other arithmetic: 7.5 us -> none  [the longest x1 6.06 us: per_device(): picked = jnp.where(live[:, :, None], picked, zero)]
  transfers between devices with their start and end apart: 3 -> 0, of which waited for: 3 -> 0; matrix products, arithmetic and copies ran while one was open for 7% -> 0% of each run, Pallas kernels for 0% -> 0%
where the time goes in v1:
time: 82.8 us; the launch traced here: 82.6 us
  Pallas kernels  80.3 us (97%)
  local copies, waits for them, and re-layouts  2.32 us (3%)
    pallas_call x1, Pallas kernels, responses(): pl.pallas_call(response_kernel, out_shape=[jax.ShapeDtypeStruct((WIDE, LA...  68.3 us
    pallas_call x1, Pallas kernels, spectra(): pl.pallas_call(spectra_kernel, grid=(LANES // step,), out_shape=jax.Shape...  11.9 us
    unnamed x4, local copies, waits for them, and re-layouts  2.32 us

profile of v1, /device:TPU:1, one launch (start us, length us, event | category | flops | bytes accessed | tf_op | source)
XLA Modules:
  0.0 82.6 jit_solution(3641471270036623546)
XLA Ops:
  0.0 68.3 %responses.1 = (bf16[768,2048]{1,0:T(8,128)(2,1)S(1)}, bf16[6,128,128]{2,1,0:T(8,128)(2,1)S(1)}) custom-call(s32[1024]{0:T(1024)} %bitcast.5, s32[1024]{0:T(1024)} %off_hbm.1, s32[1024]{0:T(1024)} %cnt_hbm.1, bf16[100,8192]{1,0:T(8,128)(2,1)} %bitcast.3, bf16[6,25,128]{2,1,0:T(8,128)(2,1)} %bitcast.4, bf16[6,64,128]{2,1,0:T(8,128)(2,1)} %psd_hbm.1), custom_call_target="tpu_custom_call" | custom-call | tf_op jit(solution)/shard_map/responses/pallas_call | solution.py:313
  68.3 0.0 copy-start
  68.4 1.6 %copy-done = bf16[768,2048]{1,0:T(8,128)(2,1)} copy-done((bf16[768,2048]{1,0:T(8,128)(2,1)}, bf16[768,2048]{1,0:T(8,128)(2,1)S(1)}, u32[]{:S(2)}) %copy-start) | copy-done | bytes 3145752
  70.0 0.0 copy-start.1
  70.0 0.7 copy-done.1
  70.7 11.9 %spectra.1 = bf16[32,6,64,128]{3,2,1,0:T(8,128)(2,1)} custom-call(bf16[768,2048]{1,0:T(8,128)(2,1)} %copy-done, bf16[6,128,128]{2,1,0:T(8,128)(2,1)} %copy-done.1), custom_call_target="tpu_custom_call" | custom-call | tf_op jit(solution)/shard_map/spectra/pallas_call | solution.py:372
Async XLA Ops:
  68.3 1.7 %copy-start = (bf16[768,2048]{1,0:T(8,128)(2,1)}, bf16[768,2048]{1,0:T(8,128)(2,1)S(1)}, u32[]{:S(2)}) copy-start(bf16[768,2048]{1,0:T(8,128)(2,1)S(1)} %get-tuple-element.7.resp_ref) | copy-start | bytes 9437188
  70.0 0.7 copy-start.1

commit v2 on v1

v2 whole, which is shorter than its diff:
```python
import functools

import jax
import jax.numpy as jnp
from jax import lax
from jax.experimental import pallas as pl
from jax.experimental.pallas import tpu as pltpu
from jax.sharding import PartitionSpec as P

MESH = pl.DeviceIdType.MESH
MODES = 800
NI = 64
PROW = 64
FREQ_DEV = 6
PAN_DEV = 32
NF = 8
NZ = 8
NX = 4
NS = NZ * NX
LOCAL = MODES // NF
SHARD = MODES // NS
CHUNKS = ((0, 32), (32, 32), (64, 32), (96, 16))
PLACES = ((0, 0), (0, 256), (1, 0), (1, 256))
DEEP = (512, 384)
PADDED = 112
LANES = PAN_DEV * PROW
WIDE = FREQ_DEV * 2 * NI
TSH = 32
f32 = jnp.float32
bf16 = jnp.bfloat16


def div(a, b):
    return lax.div(a, jnp.int32(b))


def rem(a, b):
    return lax.rem(a, jnp.int32(b))


def response_kernel(
    sup_hbm, off_hbm, cnt_hbm, table_hbm, t_hbm, psd_hbm, resp_ref, blocks_ref,
    sup, off, cnt, t_ref, psd_ref, in_sem, table, send_buf, rb0, rb1, rb2, rb3, xg0, xg1, tg0, tg1,
    tbuf, tin, acc, ranks,
    table_sem, a2a_send, a2a_recv, y_send, y_recv, tz_send, tz_recv, tx_send, tx_recv,
):
    rbs, xgs, tgs = (rb0, rb1, rb2, rb3), (xg0, xg1), (tg0, tg1)
    f = lax.axis_index("freq")
    me = lax.axis_index("se")
    z, x = div(me, NX), rem(me, NX)
    up, down = rem(f + 2, NF), rem(f + NF - 2, NF)
    across = rem(f + 4, NF)
    twin = f + 1 - 2 * rem(f, 2)
    x_up, x_down = rem(x + 1, NX), rem(x + NX - 1, NX)

    barrier = pltpu.get_barrier_semaphore()

    @pl.loop(1, NS)
    def _(i):
        pl.semaphore_signal(barrier, 1, device_id={"se": rem(me + i, NS)}, device_id_type=MESH)

    for g in (up, down, across, twin):
        pl.semaphore_signal(barrier, 1, device_id={"freq": g}, device_id_type=MESH)

    small = [
        pltpu.make_async_copy(source, to, in_sem.at[k])
        for k, (source, to) in enumerate(
            ((t_hbm, t_ref), (sup_hbm, sup), (off_hbm, off), (cnt_hbm, cnt), (psd_hbm, psd_ref))
        )
    ]
    for copy in small:
        copy.start()
    tiles = table.shape[0]

    @pl.loop(0, tiles)
    def _(t):
        part = table_hbm.at[:, pl.ds(pl.multiple_of(t * 128, 128), 128)]
        pltpu.make_async_copy(part, table.at[t], table_sem).start()

    tin[...] = jnp.zeros_like(tin)
    small[0].wait()
    tin[:, 0:SHARD, :] = t_ref[...]
    tbuf[x, z] = tin[...]
    send_buf[:, PADDED - 16 : PADDED, :] = jnp.zeros((NS, 16, 128), bf16)

    pl.semaphore_wait(barrier, NS - 1 + 4)

    def tz_at(d):
        return rem(z + NZ + d, NZ)

    def tz_copy(step, k):
        half = FREQ_DEV // 2
        if step == 0:
            source, d = tbuf.at[x, z], (1, -1, 2, -2)[k]
        else:
            source, d = (
                (tbuf.at[x, tz_at(-2)], 1),
                (tbuf.at[x, tz_at(2)], -1),
                (tbuf.at[x, tz_at(-2), 0:half], 2),
                (tbuf.at[x, tz_at(2), half:FREQ_DEV], -2),
            )[k]
        return pltpu.make_async_remote_copy(
            src_ref=source, dst_ref=source, send_sem=tz_send.at[step], recv_sem=tz_recv.at[step],
            device_id={"se": tz_at(d) * NX + x}, device_id_type=MESH,
        )

    def tz_start(step):
        for k in range(4):
            tz_copy(step, k).start()

    def tz_wait(semaphores, step):
        some = tbuf.at[0, 0 : 4 - step]
        pltpu.make_async_copy(some, some, semaphores.at[step]).wait()

    tz_start(0)

    lane = lax.broadcasted_iota(jnp.int32, (LOCAL, 128), 1)

    def window(start, place):
        tile = div(start, 128)
        inside = start - tile * 128
        a = table[tile].astype(f32)
        b = table[jnp.minimum(tile + 1, tiles - 1)].astype(f32)
        both = jnp.where(lane >= inside, a, b)
        return pltpu.roll(both, rem(place + 128 - inside, 128), 1)

    def gather(o):
        base = o * PAN_DEV
        first, last = jnp.int32(0), jnp.int32(0)
        hits = [sup[base + j] == me for j in range(PAN_DEV)]
        starts = [off[base + j] for j in range(PAN_DEV)]
        for j in range(PAN_DEV):
            last = jnp.where(hits[j], starts[j], last)
            k = PAN_DEV - 1 - j
            first = jnp.where(hits[k], starts[k], first)
        got = jnp.where(lane < PROW, window(first, 0), window(last, PROW)).astype(bf16)
        send_buf[o, 0:LOCAL, :] = got

    def a2a_copy(c, o):
        r0, rows = CHUNKS[c]
        return pltpu.make_async_remote_copy(
            src_ref=send_buf.at[o, pl.ds(r0, rows)], dst_ref=rbs[c].at[me],
            send_sem=a2a_send.at[c], recv_sem=a2a_recv.at[c],
            device_id={"se": o}, device_id_type=MESH,
        )

    def a2a_start(c):
        @pl.loop(1, NS)
        def _(i):
            a2a_copy(c, rem(me + i, NS)).start()

    def a2a_sent(c):
        sent = rbs[c].at[0 : NS - 1]
        pltpu.make_async_copy(sent, sent, a2a_send.at[c]).wait()

    small[1].wait()
    small[2].wait()
    pltpu.make_async_copy(table, table, table_sem).wait()
    @pl.loop(0, NS, unroll=4)
    def _(o):
        gather(o)

    tz_wait(tz_recv, 0)
    tz_start(1)
    for c in range(len(CHUNKS)):
        a2a_start(c)
    for c, (r0, rows) in enumerate(CHUNKS):
        rbs[c][me] = send_buf[me, r0 : r0 + rows, :]

    def tx_copy(k):
        half = NZ // 2
        source, to = (
            (tbuf.at[x, 0:half], x_up),
            (tbuf.at[x, half:NZ], x_down),
            (tbuf.at[x, half:NZ], x_up),
            (tbuf.at[x, 0:half], x_down),
            (tbuf.at[x_down, 0:half], x_up),
            (tbuf.at[x_up, half:NZ], x_down),
        )[k]
        return pltpu.make_async_remote_copy(
            src_ref=source, dst_ref=source, send_sem=tx_send.at[k], recv_sem=tx_recv.at[k],
            device_id={"se": z * NX + to}, device_id_type=MESH,
        )

    tz_wait(tz_recv, 1)
    for k in range(4):
        tx_copy(k).start()

    small[3].wait()
    small[4].wait()
    half_lane = lax.broadcasted_iota(jnp.int32, (NI, 128), 1)
    i = lax.broadcasted_iota(jnp.int32, (128, 128), 0)
    j = lax.broadcasted_iota(jnp.int32, (128, 128), 1)
    swap = jnp.where(j == i + NI, 1.0, jnp.where(i == j + NI, -1.0, 0.0)).astype(bf16)
    for g in range(FREQ_DEV):
        turned = pltpu.roll(psd_ref[g].astype(f32), NI, 1)
        blocks_ref[g, 0:NI, 0:128] = psd_ref[g]
        blocks_ref[g, NI:128, 0:128] = jnp.where(half_lane < NI, -turned, turned).astype(bf16)
        blocks_ref[g, :, 128:256] = swap

    mine = me * PAN_DEV
    own = [sup[mine + p] for p in range(PAN_DEV)]
    for p in range(PAN_DEV):
        rank = jnp.int32(0)
        for e in range(p):
            rank = jnp.where(own[e] == own[p], 1, rank)
        ranks[p] = rank

    def rows_at(c, slot):
        rows = CHUNKS[c][1]
        return pl.ds(pl.multiple_of(PLACES[c][1] + slot * rows, 16), rows)

    def select(c):
        rows = CHUNKS[c][1]
        all_c = rbs[c].at[0 : NS - 1]
        pltpu.make_async_copy(all_c, all_c, a2a_recv.at[c]).wait()
        at = lax.broadcasted_iota(jnp.int32, (rows, 128), 1)

        @pl.loop(0, PAN_DEV // 2, unroll=4)
        def _(q):
            p = 2 * q
            left = rbs[c][sup[mine + p]].astype(f32)
            right = rbs[c][sup[mine + p + 1]].astype(f32)
            left = pltpu.roll(left, PROW * ranks[p], 1)
            right = pltpu.roll(right, PROW * (1 - ranks[p + 1]), 1)
            live = jnp.where(at < PROW, cnt[mine + p], cnt[mine + p + 1] + PROW)
            pair = jnp.where(at < live, jnp.where(at < PROW, left, right), 0.0)
            xgs[PLACES[c][0]][rows_at(c, f), pl.ds(pl.multiple_of(q * 128, 128), 128)] = pair.astype(bf16)

    def y_copy(c, k):
        slot, to = ((f, up), (f, down), (f, across), (f, twin), (down, twin), (up, twin), (across, twin))[k]
        source = xgs[PLACES[c][0]].at[rows_at(c, slot)]
        return pltpu.make_async_remote_copy(
            src_ref=source, dst_ref=source, send_sem=y_send.at[c, k], recv_sem=y_recv.at[c, k],
            device_id={"freq": to}, device_id_type=MESH,
        )

    def y_begin(c):
        for k in range(4):
            y_copy(c, k).start()

    def y_relay(c):
        for k in range(3):
            y_copy(c, k).wait_recv()
            y_copy(c, k + 4).start()

    def y_end(c):
        for k in range(3, 7):
            y_copy(c, k).wait_recv()

    def tx_forward():
        for k in (0, 1):
            tx_copy(k).wait_recv()
            tx_copy(k + 4).start()

    def tx_end():
        for k in (2, 3, 4, 5):
            tx_copy(k).wait_recv()

    def compact():
        k = lax.broadcasted_iota(jnp.int32, (PADDED, 128), 0)
        at = lax.broadcasted_iota(jnp.int32, (PADDED, 128), 1)
        mode = jnp.where(rem(at, TSH) < SHARD, div(at, TSH) * SHARD + rem(at, TSH), -1)
        pick = jnp.where(k == mode, 1.0, 0.0).astype(bf16)

        @pl.loop(0, NZ)
        def _(zz):
            blocks = [tbuf[:, zz, g].reshape(NX * TSH, 128) for g in range(FREQ_DEV)]
            rows_of = jnp.dot(pick, jnp.concatenate(blocks, axis=1), preferred_element_type=f32).astype(bf16)
            for c, (r0, rows) in enumerate(CHUNKS):
                tgs[PLACES[c][0]][rows_at(c, zz), :] = rows_of[r0 : r0 + rows]

    def multiply(group):
        step = 512

        @pl.loop(0, LANES // step)
        def _(n):
            at = pl.ds(pl.multiple_of(n * step, step), step)
            part = lax.dot_general(
                xgs[group][:, at], tgs[group][...], (((0,), (0,)), ((), ())), preferred_element_type=f32
            )
            if group == 0:
                acc[at, :] = part
            else:
                resp_ref[at, :] = (acc[at, :] + part).astype(bf16)

    select(0)
    y_begin(0)
    tx_forward()
    select(1)
    y_begin(1)
    y_relay(0)
    select(2)
    y_begin(2)
    tx_end()
    compact()
    y_relay(1)
    select(3)
    y_begin(3)
    y_end(0)
    y_end(1)
    multiply(0)
    y_relay(2)
    y_relay(3)
    y_end(2)
    y_end(3)
    multiply(1)

    tz_wait(tz_send, 0)
    tz_wait(tz_send, 1)
    for c in range(len(CHUNKS)):
        a2a_sent(c)
    for k in range(6):
        tx_copy(k).wait_send()
    for c in range(len(CHUNKS)):
        for k in range(7):
            y_copy(c, k).wait_send()


def responses(sup, off, cnt, table, transfer, psd):
    return pl.pallas_call(
        response_kernel,
        out_shape=[
            jax.ShapeDtypeStruct((LANES, WIDE), bf16),
            jax.ShapeDtypeStruct((FREQ_DEV, 128, 256), bf16),
        ],
        in_specs=[pl.BlockSpec(memory_space=pltpu.HBM)] * 6,
        out_specs=[pl.BlockSpec(memory_space=pltpu.VMEM)] * 2,
        scratch_shapes=[
            *[pltpu.SMEM(a.shape, jnp.int32) for a in (sup, off, cnt)],
            pltpu.VMEM(transfer.shape, bf16),
            pltpu.VMEM(psd.shape, bf16),
            pltpu.SemaphoreType.DMA((5,)),
            pltpu.VMEM((table.shape[1] // 128, LOCAL, 128), bf16),
            pltpu.VMEM((NS, PADDED, 128), bf16),
            *[pltpu.VMEM((NS, rows, 128), bf16) for _, rows in CHUNKS],
            *[pltpu.VMEM((deep, LANES), bf16) for deep in DEEP],
            *[pltpu.VMEM((deep, WIDE), bf16) for deep in DEEP],
            pltpu.VMEM((NX, NZ, FREQ_DEV, TSH, 128), bf16),
            pltpu.VMEM((FREQ_DEV, TSH, 128), bf16),
            pltpu.VMEM((LANES, WIDE), f32),
            pltpu.SMEM((PAN_DEV,), jnp.int32),
            pltpu.SemaphoreType.DMA,
            pltpu.SemaphoreType.DMA((len(CHUNKS),)),
            pltpu.SemaphoreType.DMA((len(CHUNKS),)),
            pltpu.SemaphoreType.DMA((len(CHUNKS), 7)),
            pltpu.SemaphoreType.DMA((len(CHUNKS), 7)),
            pltpu.SemaphoreType.DMA((2,)),
            pltpu.SemaphoreType.DMA((2,)),
            pltpu.SemaphoreType.DMA((6,)),
            pltpu.SemaphoreType.DMA((6,)),
        ],
        compiler_params=pltpu.CompilerParams(
            collective_id=0, has_side_effects=True, vmem_limit_bytes=44 * 2**20
        ),
        name="responses",
    )(*[pltpu.with_memory_space_constraint(a, pltpu.HBM) for a in (sup, off, cnt, table, transfer, psd)])


def spectra_kernel(resp_ref, blocks_ref, out_ref):
    for g in range(FREQ_DEV):
        resp = resp_ref[:, g * 128 : (g + 1) * 128]
        both = jnp.dot(resp, blocks_ref[g], preferred_element_type=f32).astype(bf16)
        for h in range(0, out_ref.shape[0], 2):
            one = slice(h * PROW, (h + 1) * PROW)
            two = slice((h + 1) * PROW, (h + 2) * PROW)
            pair = slice(h * PROW, (h + 2) * PROW)
            other = jnp.concatenate([resp[one], both[one, 128:256], resp[two], both[two, 128:256]], axis=0)
            cross = lax.dot_general(
                both[pair, 0:128], other, (((1,), (1,)), ((), ())), preferred_element_type=f32
            )
            out_ref[h, g] = cross[0:PROW, 0:128].astype(bf16)
            out_ref[h + 1, g] = cross[PROW:, 128:256].astype(bf16)


def spectra(resp, blocks):
    step = 512
    return pl.pallas_call(
        spectra_kernel,
        grid=(LANES // step,),
        out_shape=jax.ShapeDtypeStruct((PAN_DEV, FREQ_DEV, PROW, 2 * NI), bf16),
        in_specs=[
            pl.BlockSpec((step, WIDE), lambda i: (i, 0)),
            pl.BlockSpec((FREQ_DEV, 128, 256), lambda i: (0, 0, 0)),
        ],
        out_specs=pl.BlockSpec((step // PROW, FREQ_DEV, PROW, 2 * NI), lambda i: (i, 0, 0, 0)),
        compiler_params=pltpu.CompilerParams(vmem_limit_bytes=16 * 2**20),
        name="spectra",
    )(resp, blocks)


def per_device(stress_modes, modal_transfer, input_psd, panel_super, panel_offset, panel_count):
    resp, blocks = responses(
        panel_super.reshape(-1), panel_offset, panel_count,
        stress_modes.T, modal_transfer.transpose(1, 0, 2), input_psd,
    )
    return spectra(resp, blocks)


def solution(mesh):
    in_specs = (P("se", "freq"), P("se", "freq", None), P("freq", None, None), P(), P(), P())
    out_specs = P("se", "freq", None, None)
    return jax.shard_map(
        per_device, mesh=mesh, in_specs=in_specs, out_specs=out_specs, check_vma=False
    )
```

time: 82.8 us -> 59.2 us (0.71)
  Pallas kernels: 80.3 us -> 59 us
  local copies, waits for them, and re-layouts: 2.32 us -> 0 us
    pallas_call x1, Pallas kernels: 68.3 us -> 53.7 us  [responses(): pl.pallas_call(response_kernel, out_shape=[jax.ShapeDtypeStruct((LANES, W...]
    pallas_call x1, Pallas kernels: 11.9 us -> 5.32 us  [spectra(): pl.pallas_call(spectra_kernel, grid=(LANES // step,), out_shape=jax.Shape...]
    unnamed x4 -> x0, local copies, waits for them, and re-layouts: 2.32 us -> none
where the time goes in v2:
time: 59.2 us; the launch traced here: 59 us
  Pallas kernels  59 us (100%)
    pallas_call x1, Pallas kernels, responses(): pl.pallas_call(response_kernel, out_shape=[jax.ShapeDtypeStruct((LANES, W...  53.7 us
    pallas_call x1, Pallas kernels, spectra(): pl.pallas_call(spectra_kernel, grid=(LANES // step,), out_shape=jax.Shape...  5.32 us

profile of v2, /device:TPU:1, one launch (start us, length us, event | category | flops | bytes accessed | tf_op | source)
XLA Modules:
  0.0 59.0 jit_solution(5549835029091564201)
XLA Ops:
  0.0 53.7 %responses.1 = (bf16[2048,768]{1,0:T(8,128)(2,1)S(1)}, bf16[6,128,256]{2,1,0:T(8,128)(2,1)S(1)}) custom-call(s32[1024]{0:T(1024)} %bitcast.5, s32[1024]{0:T(1024)} %off_hbm.1, s32[1024]{0:T(1024)} %cnt_hbm.1, bf16[100,8192]{1,0:T(8,128)(2,1)} %bitcast.3, bf16[6,25,128]{2,1,0:T(8,128)(2,1)} %bitcast.4, bf16[6,64,128]{2,1,0:T(8,128)(2,1)} %psd_hbm.1), custom_call_target="tpu_custom_call" | custom-call | tf_op jit(solution)/shard_map/responses/pallas_call | solution.py:321
  53.7 5.3 %spectra.1 = bf16[32,6,64,128]{3,2,1,0:T(8,128)(2,1)} custom-call(bf16[2048,768]{1,0:T(8,128)(2,1)S(1)} %get-tuple-element.7.resp_ref, bf16[6,128,256]{2,1,0:T(8,128)(2,1)S(1)} %get-tuple-element.8.blocks_ref), custom_call_target="tpu_custom_call" | custom-call | tf_op jit(solution)/shard_map/spectra/pallas_call | solution.py:378

commit v3 on v2

--- a/solution.py
+++ b/solution.py
@@ -263,7 +263,7 @@
         mode = jnp.where(rem(at, TSH) < SHARD, div(at, TSH) * SHARD + rem(at, TSH), -1)
         pick = jnp.where(k == mode, 1.0, 0.0).astype(bf16)
 
-        @pl.loop(0, NZ)
+        @pl.loop(0, NZ, unroll=2)
         def _(zz):
             blocks = [tbuf[:, zz, g].reshape(NX * TSH, 128) for g in range(FREQ_DEV)]
             rows_of = jnp.dot(pick, jnp.concatenate(blocks, axis=1), preferred_element_type=f32).astype(bf16)
@@ -292,11 +292,11 @@
     y_relay(0)
     select(2)
     y_begin(2)
-    tx_end()
-    compact()
     y_relay(1)
     select(3)
     y_begin(3)
+    tx_end()
+    compact()
     y_end(0)
     y_end(1)
     multiply(0)
@@ -374,7 +374,7 @@
 
 
 def spectra(resp, blocks):
-    step = 512
+    step = 1024
     return pl.pallas_call(
         spectra_kernel,
         grid=(LANES // step,),

time: 59.2 us -> 59.1 us (level)
  no operation moved by 1% of the time
where the time goes in v3:
time: 59.1 us; the launch traced here: 58.9 us
  Pallas kernels  58.9 us (100%)
    pallas_call x1, Pallas kernels, responses(): pl.pallas_call(response_kernel, out_shape=[jax.ShapeDtypeStruct((LANES, W...  53.9 us
    pallas_call x1, Pallas kernels, spectra(): pl.pallas_call(spectra_kernel, grid=(LANES // step,), out_shape=jax.Shape...  5.01 us

profile of v3, /device:TPU:1, one launch (start us, length us, event | category | flops | bytes accessed | tf_op | source)
XLA Modules:
  0.0 58.9 jit_solution(378772815410949884)
XLA Ops:
  0.0 53.9 %responses.1 = (bf16[2048,768]{1,0:T(8,128)(2,1)S(1)}, bf16[6,128,256]{2,1,0:T(8,128)(2,1)S(1)}) custom-call(s32[1024]{0:T(1024)} %bitcast.5, s32[1024]{0:T(1024)} %off_hbm.1, s32[1024]{0:T(1024)} %cnt_hbm.1, bf16[100,8192]{1,0:T(8,128)(2,1)} %bitcast.3, bf16[6,25,128]{2,1,0:T(8,128)(2,1)} %bitcast.4, bf16[6,64,128]{2,1,0:T(8,128)(2,1)} %psd_hbm.1), custom_call_target="tpu_custom_call" | custom-call | tf_op jit(solution)/shard_map/responses/pallas_call | solution.py:321
  53.9 5.0 %spectra.1 = bf16[32,6,64,128]{3,2,1,0:T(8,128)(2,1)} custom-call(bf16[2048,768]{1,0:T(8,128)(2,1)S(1)} %get-tuple-element.7.resp_ref, bf16[6,128,256]{2,1,0:T(8,128)(2,1)S(1)} %get-tuple-element.8.blocks_ref), custom_call_target="tpu_custom_call" | custom-call | tf_op jit(solution)/shard_map/spectra/pallas_call | solution.py:378
